TPU v7x, 32 devices: a whole 2x2x4 slice. The times are simulated.
32 devices in a mesh: dp: 8 (over z, y), chan: 4 (over x, core).
Axes of the slice: x: 2, y: 2, z: 4, core: 2. Of those that a mesh axis runs over, the one named last changes fastest.
Arguments:
- mel: bfloat16 [16, 2816, 80], P('dp', 'chan'), may hold values from -6 to 6
- lang_group: int32 [16], P('dp'), may hold values from 0 to 15
- clip_count: int32 [8], replicated, may hold values from 1 to 2, as said below
- conv_one: bfloat16 [240, 768], P(None, 'chan'), may hold values from -0.375 to 0.375
- conv_one_bias: bfloat16 [768], P('chan'), may hold values from -1.796875 to 1.796875
- conv_two: bfloat16 [3, 768, 768], P(None, 'chan'), may hold values from -0.125 to 0.125
- conv_two_bias: bfloat16 [768], replicated, may hold values from -1.796875 to 1.796875
- lang_table: bfloat16 [16, 768], replicated, may hold values from -3 to 3
- ln_one_gain: bfloat16 [768], replicated, may hold values from 0.5 to 1.5
- ln_one_bias: bfloat16 [768], replicated, may hold values from -1.796875 to 1.796875
- w_qkv: bfloat16 [768, 2304], P('chan'), may hold values from -0.3125 to 0.3125
- q_bias: bfloat16 [768], replicated, may hold values from -1.796875 to 1.796875
- v_bias: bfloat16 [768], replicated, may hold values from -1.796875 to 1.796875
- w_out: bfloat16 [768, 768], P('chan'), may hold values from -0.875 to 0.875
- out_bias: bfloat16 [768], replicated, may hold values from -1.796875 to 1.796875
- ln_two_gain: bfloat16 [768], replicated, may hold values from 0.5 to 1.5
- ln_two_bias: bfloat16 [768], replicated, may hold values from -1.796875 to 1.796875
- w_fc_one: bfloat16 [768, 3072], P('chan'), may hold values from -0.21875 to 0.21875
- fc_one_bias: bfloat16 [3072], replicated, may hold values from -1.796875 to 1.796875
- w_fc_two: bfloat16 [3072, 768], P('chan'), may hold values from -0.109375 to 0.109375
- fc_two_bias: bfloat16 [768], replicated, may hold values from -1.796875 to 1.796875
- grad_out: bfloat16 [16, 1408, 768], P('dp', 'chan'), may hold values from -6 to 6
Outputs:
- encoded: bfloat16 [16, 1408, 768], P('dp', 'chan')
- mel_grad: float32 [16, 2816, 80], P('dp', 'chan')
- conv_one_grad: float32 [240, 768], P(None, 'chan')
- conv_one_bias_grad: float32 [768], P('chan')
- conv_two_grad: float32 [3, 768, 768], P(None, 'chan')
- conv_two_bias_grad: float32 [768], replicated
- lang_table_grad: float32 [16, 768], replicated
- ln_one_gain_grad: float32 [768], replicated
- ln_one_bias_grad: float32 [768], replicated
- w_qkv_grad: float32 [768, 2304], P('chan')
- q_bias_grad: float32 [768], replicated
- v_bias_grad: float32 [768], replicated
- w_out_grad: float32 [768, 768], P('chan')
- out_bias_grad: float32 [768], replicated
- ln_two_gain_grad: float32 [768], replicated
- ln_two_bias_grad: float32 [768], replicated
- w_fc_one_grad: float32 [768, 3072], P('chan')
- fc_one_bias_grad: float32 [3072], replicated
- w_fc_two_grad: float32 [3072, 768], P('chan')
- fc_two_bias_grad: float32 [768], replicated
Inputs may be any that keep to these rules, and one draw needn't show every extreme that they name: Slot s of index i of dp holds a live clip when s < clip_count[i]; some index has 2 live clips and some has 1.
All inputs are finite; a program needn't handle non-finite values.
Results may differ from a plain program's by a relative error of at most 0.02.
Values may be sent and summed in bfloat16 or wider, within the bound.
No kernel may reach another device: no remote copies, remote signals or barrier semaphores. Data moves between devices by JAX's collectives and lax.ppermute only.
A program may use at most 320 MiB of HBM per device.

v0:
```python
import math

import jax
import jax.numpy as jnp
from jax import lax
from jax.experimental import pallas as pl
from jax.experimental.pallas import tpu as pltpu
from jax.sharding import PartitionSpec as P

HEAD_DIM = 64
PAIR = 2 * HEAD_DIM
SCALE = HEAD_DIM ** (-0.5)
BF16 = jnp.bfloat16
F32 = jnp.float32

CORE = [(j, j ^ 1) for j in range(4)]
CROSS = [(j, j ^ 2) for j in range(4)]
SAME = [(2 * x + c, 2 * c + x) for x in range(2) for c in range(2)]
OTHER = [(2 * x + c, 2 * (1 - c) + x) for x in range(2) for c in range(2)]
SAME_BACK = [(b, a) for a, b in SAME]
OTHER_BACK = [(b, a) for a, b in OTHER]


def send(block, perm):
    return lax.ppermute(block, "chan", perm)


def ordered(first_is_own, own, other, axis=0, stack=False):
    join = jnp.stack if stack else jnp.concatenate
    return jnp.where(first_is_own, join([own, other], axis), join([other, own], axis))


def pick(block, index, axis):
    return lax.dynamic_index_in_dim(block, index, axis, keepdims=False)


def gelu_both(inputs):
    cdf = 0.5 * (1.0 + lax.erf(inputs * math.sqrt(0.5)))
    pdf = jnp.exp(-0.5 * inputs * inputs) * (1.0 / math.sqrt(2.0 * math.pi))
    return inputs * cdf, cdf + inputs * pdf


def norm_stats(inputs):
    row_mean = jnp.mean(inputs, axis=-1, keepdims=True)
    centered = inputs - row_mean
    variance = jnp.mean(centered * centered, axis=-1, keepdims=True)
    return row_mean, lax.rsqrt(variance + 1e-05)


def norm_back(inputs, stats, gain_vec, cotangent):
    row_mean, inverse = stats
    unit = (inputs - row_mean) * inverse
    scaled = cotangent * gain_vec
    mean_one = jnp.mean(scaled, axis=-1, keepdims=True)
    mean_two = jnp.mean(scaled * unit, axis=-1, keepdims=True)
    grad = inverse * (scaled - mean_one - unit * mean_two)
    return grad, jnp.sum(cotangent * unit, axis=0), jnp.sum(cotangent, axis=0)


def positions(frame_count, model_width, first_frame):
    increment = math.log(10000.0) / (model_width // 2 - 1)
    inverse = jnp.exp(-increment * jnp.arange(model_width // 2, dtype=jnp.float32))
    angles = (first_frame + jnp.arange(frame_count)).astype(jnp.float32)[:, None] * inverse[None, :]
    return jnp.concatenate([jnp.sin(angles), jnp.cos(angles)], axis=1)


def mm(left, right):
    return jnp.dot(left, right, preferred_element_type=F32)


def mm_nt(left, right):
    return lax.dot_general(left, right, (((1,), (1,)), ((), ())), preferred_element_type=F32)


def mm_tn(left, right):
    return lax.dot_general(left, right, (((0,), (0,)), ((), ())), preferred_element_type=F32)


def head_stack(block):
    lane = lax.broadcasted_iota(jnp.int32, block.shape, 1)
    zero = jnp.zeros_like(block)
    return jnp.concatenate(
        [jnp.where(lane < HEAD_DIM, block, zero), jnp.where(lane < HEAD_DIM, zero, block)], axis=0
    )


def head_join(stacked):
    rows = stacked.shape[0] // 2
    lane = lax.broadcasted_iota(jnp.int32, (rows, stacked.shape[1]), 1)
    return jnp.where(lane < HEAD_DIM, stacked[:rows], stacked[rows:])


def attend_kernel(chunk, q_ref, k_own, k_oth, v_own, v_oth, *refs):
    att_ref, lse_ref, k_all, v_all = refs[-4:]
    rows = q_ref.shape[0]
    k_all[0:rows] = k_own[...]
    k_all[rows:] = k_oth[...]
    v_all[0:rows, 0:PAIR] = v_own[...]
    v_all[rows:, 0:PAIR] = v_oth[...]
    v_all[:, PAIR:] = jnp.ones((2 * rows, PAIR), BF16)
    for start in range(0, rows, chunk):
        at = pl.ds(start, chunk)
        queries = head_stack(q_ref[at] * SCALE)
        scores = mm_nt(queries, k_all[...])
        top = jnp.max(scores, axis=1, keepdims=True)
        both = mm(jnp.exp(scores - top).astype(BF16), v_all[...])
        total = both[:, PAIR:]
        att_ref[at] = head_join(both[:, :PAIR] / total).astype(BF16)
        lse_ref[at] = head_join(top + jnp.log(total))


def attend(q, kv_own, kv_oth, first, count, pairs, earlier=()):
    rows = q.shape[0]
    chunk = 176
    spec = lambda shift: pl.BlockSpec((rows, PAIR), lambda p: (0, p + shift))
    return pl.pallas_call(
        lambda *refs: attend_kernel(chunk, *refs),
        grid=(count,),
        in_specs=[spec(first), spec(first), spec(first), spec(first + pairs), spec(first + pairs)]
        + [pl.BlockSpec(memory_space=pl.ANY)] * len(earlier),
        out_specs=[spec(first)] * 2,
        out_shape=[
            jax.ShapeDtypeStruct((rows, pairs * PAIR), BF16),
            jax.ShapeDtypeStruct((rows, pairs * PAIR), F32),
        ],
        input_output_aliases={5 + i: i for i in range(len(earlier))},
        scratch_shapes=[
            pltpu.VMEM((2 * rows, PAIR), BF16),
            pltpu.VMEM((2 * rows, 2 * PAIR), BF16),
        ],
        compiler_params=pltpu.CompilerParams(vmem_limit_bytes=56 * 1024 * 1024),
        cost_estimate=pl.CostEstimate(
            flops=count * 16 * rows * rows * PAIR,
            bytes_accessed=count * PAIR * rows * 16,
            transcendentals=4 * count * rows * rows,
        ),
        name="attend",
    )(q, kv_own, kv_oth, kv_own, kv_oth, *earlier)


def attend_back_kernel(chunk, q_ref, k_own, k_oth, v_own, v_oth, lse_ref, g_ref, *refs):
    dq_ref, own_ref, oth_ref, k_all, v_all, q_all, g_all, p_all, s_all = refs[-9:]
    rows = q_ref.shape[0]
    k_all[0:rows] = k_own[...]
    k_all[rows:] = k_oth[...]
    v_all[0:rows] = v_own[...]
    v_all[rows:] = v_oth[...]
    for start in range(0, rows, chunk):
        at = pl.ds(start, chunk)
        both = pl.ds(2 * start, 2 * chunk)
        queries = head_stack(q_ref[at] * SCALE)
        grads = head_stack(g_ref[at])
        q_all[both] = queries
        g_all[both] = grads
        lse = jnp.concatenate([lse_ref[at, 0:1], lse_ref[at, HEAD_DIM : HEAD_DIM + 1]], axis=0)
        probs = jnp.exp(mm_nt(queries, k_all[...]) - lse)
        grad_probs = mm_nt(grads, v_all[...])
        inner = jnp.sum(probs * grad_probs, axis=1, keepdims=True)
        grad_scores = (probs * (grad_probs - inner)).astype(BF16)
        p_all[both] = probs.astype(BF16)
        s_all[both] = grad_scores
        dq_ref[at] = (head_join(mm(grad_scores, k_all[...])) * SCALE).astype(BF16)

    dk = mm_tn(q_all[...], s_all[...]).T.astype(BF16)
    own_ref[0] = dk[0:rows]
    oth_ref[0] = dk[rows:]
    dv = mm_tn(g_all[...], p_all[...]).T.astype(BF16)
    own_ref[1] = dv[0:rows]
    oth_ref[1] = dv[rows:]


def attend_back(q, kv_own, kv_oth, lse, grad_att, first, count, pairs, earlier=()):
    rows = q.shape[0]
    chunk = 176
    spec = lambda shift: pl.BlockSpec((rows, PAIR), lambda p: (0, p + shift))
    two = pl.BlockSpec((2, rows, PAIR), lambda p: (0, 0, p + first))
    both = jax.ShapeDtypeStruct((2, rows, pairs * PAIR), BF16)
    return pl.pallas_call(
        lambda *refs: attend_back_kernel(chunk, *refs),
        grid=(count,),
        in_specs=[spec(first), spec(first), spec(first), spec(first + pairs), spec(first + pairs)]
        + [spec(first)] * 2
        + [pl.BlockSpec(memory_space=pl.ANY)] * len(earlier),
        out_specs=[spec(first), two, two],
        out_shape=[jax.ShapeDtypeStruct((rows, pairs * PAIR), BF16), both, both],
        input_output_aliases={7 + i: i for i in range(len(earlier))},
        scratch_shapes=[pltpu.VMEM((2 * rows, PAIR), BF16)] * 4
        + [pltpu.VMEM((2 * rows, 2 * rows), BF16)] * 2,
        compiler_params=pltpu.CompilerParams(vmem_limit_bytes=56 * 1024 * 1024),
        cost_estimate=pl.CostEstimate(
            flops=count * 40 * rows * rows * PAIR,
            bytes_accessed=count * PAIR * rows * 26,
            transcendentals=4 * count * rows * rows,
        ),
        name="attend_back",
    )(q, kv_own, kv_oth, kv_own, kv_oth, lse, grad_att, *earlier)


def join(*values):
    return lax.optimization_barrier(values)


def after(value, *others):
    return lax.optimization_barrier((value,) + others)[0]


def place_kernel(moves, halved, index_ref, own, near, *refs):
    outs = len(refs) - (3 if halved else 2) - 1
    fars, wholes, sems = refs[: -outs - 1], refs[-outs - 1 : -1], refs[-1]
    j, y = index_ref[0], index_ref[1]
    x, c = j // 2, j % 2
    rows = own.shape[1]
    across = rows * (2 * (1 - x) + c)
    beside = rows * (2 * (1 - x) + 1 - c)
    pieces = [(own, rows * j), (near, rows * (2 * x + 1 - c))]
    if halved:
        half = rows // 2
        pieces += [
            (fars[0], across + half * y),
            (fars[1], across + half * (1 - y)),
            (fars[2].at[0], beside + half * y),
            (fars[2].at[1], beside + half * (1 - y)),
        ]
    else:
        half = rows
        pieces += [(fars[0], across), (fars[1], beside)]
    copies = []
    for piece, row in pieces:
        at = pl.ds(pl.multiple_of(row, half), piece.shape[1])
        for move in moves:
            source, target = move(piece, wholes, at)
            copies.append(pltpu.make_async_copy(source, target, sems.at[len(copies)]))
    for copy in copies:
        copy.start()
    for copy in copies:
        copy.wait()


def place(index, parts, moves, *shapes):
    anywhere = pl.BlockSpec(memory_space=pl.ANY)
    halved = len(parts) == 5
    return pl.pallas_call(
        lambda *refs: place_kernel(moves, halved, *refs),
        in_specs=[pl.BlockSpec(memory_space=pltpu.SMEM)] + [anywhere] * len(parts),
        out_specs=[pl.BlockSpec(memory_space=pltpu.VMEM)] * len(shapes),
        out_shape=[jax.ShapeDtypeStruct(shape, BF16) for shape in shapes],
        scratch_shapes=[pltpu.SemaphoreType.DMA(((6 if halved else 4) * len(moves),))],
        compiler_params=pltpu.CompilerParams(vmem_limit_bytes=16 * 1024 * 1024),
        cost_estimate=pl.CostEstimate(
            flops=0, bytes_accessed=sum(4 * math.prod(shape) for shape in shapes), transcendentals=0
        ),
        name="place",
    )(index, *parts)


ROW_MOVES = [lambda piece, wholes, at: (piece.at[0], wholes[0].at[at])]
TAP_MOVES = [lambda piece, wholes, at: (piece, wholes[0].at[:, at])]


def block_moves(blocks, width):
    def move(block):
        columns = pl.ds(block * width, width)
        return lambda piece, wholes, at: (piece.at[1 + block], wholes[1].at[at, columns])

    return ROW_MOVES + [move(block) for block in range(blocks)]


def round_sum(*terms):
    return sum(term.astype(F32) for term in terms).astype(BF16)


def dp_bits():
    bits = [1]
    while 2 * bits[-1] < lax.axis_size("dp"):
        bits.append(2 * bits[-1])
    return bits


def over_dp(block, bit):
    return lax.ppermute(block, "dp", [(d, d ^ bit) for d in range(lax.axis_size("dp"))])


def dp_side(bit):
    return (lax.axis_index("dp") // bit) % 2


class Terms:
    def __init__(self, array, names):
        self.terms, self.fixed = [(array, tuple(names))], {}

    def view(self, chosen):
        def cut(array, names):
            axis = 0
            for name in names:
                if name in chosen:
                    array = pick(array, chosen[name], axis)
                else:
                    axis += 1
            return array

        return round_sum(*[cut(array, names) for array, names in self.terms])

    def hop(self, name, side, ship):
        block = self.view({**self.fixed, name: 1 - side})
        names = tuple(n for n in self.terms[0][1] if n not in self.fixed and n != name)
        self.fixed[name] = side
        self.terms.append((ship(block), names))

    def dp_hop(self, bit):
        self.hop(bit, dp_side(bit), lambda block: over_dp(block, bit))

    def quad_hop(self, pair):
        sides = [dp_side(bit) for bit in pair]
        names = tuple(n for n in self.terms[0][1] if n not in self.fixed and n not in pair)
        arrived = []
        for other in (1, 2, 3):
            place = {pair[0]: (sides[0] + other // 2) % 2, pair[1]: (sides[1] + other) % 2}
            arrived.append(quad_send(self.view({**self.fixed, **place}), pair, other))
        self.fixed.update(zip(pair, sides))
        self.terms += [(block, names) for block in arrived]

    def rest_hops(self):
        for group in rest_groups():
            if len(group) == 2:
                self.quad_hop(group)
            else:
                self.dp_hop(group[0])

    def total(self):
        return self.view(self.fixed)

    @property
    def arrays(self):
        return [array for array, _ in self.terms]

    @arrays.setter
    def arrays(self, arrays):
        self.terms = [(array, names) for array, (_, names) in zip(arrays, self.terms)]


def tie(sums, *main):
    lists, main = lax.optimization_barrier(([t.arrays for t in sums], main))
    for t, arrays in zip(sums, lists):
        t.arrays = arrays
    return main[0] if len(main) == 1 else main


class Gather:
    def __init__(self, share, axis=0):
        self.share, self.axis, self.group, self.arrived = share, axis, (), []

    def settle(self):
        sides = [dp_side(bit) == 0 for bit in self.group]
        if len(sides) == 1:
            self.share = ordered(sides[0], self.share, self.arrived[0], self.axis)
        elif len(sides) == 2:
            near, far, last = self.arrived
            own_pair = ordered(sides[1], self.share, near, self.axis)
            far_pair = ordered(sides[1], far, last, self.axis)
            self.share = ordered(sides[0], own_pair, far_pair, self.axis)
        self.group, self.arrived = (), []
        return self.share

    def hop(self, group):
        share = self.settle()
        self.group = group
        if len(group) == 1:
            self.arrived = [over_dp(share, group[0])]
        else:
            self.arrived = [quad_send(share, group, other) for other in (1, 2, 3)]

    def rest_hops(self):
        for group in reversed(rest_groups()):
            self.hop(group)

    @property
    def arrays(self):
        return [self.share] + self.arrived

    @arrays.setter
    def arrays(self, arrays):
        self.share, self.arrived = arrays[0], list(arrays[1:])


def rest_groups():
    bits = dp_bits()[1:]
    return [tuple(bits[k : k + 2]) for k in range(0, len(bits), 2)]


def quad_send(block, pair, other):
    flip = pair[0] * (other // 2) + pair[1] * (other % 2)
    return lax.ppermute(block, "dp", [(d, d ^ flip) for d in range(lax.axis_size("dp"))])


def on_device(
    mel,
    lang_group,
    clip_count,
    conv_one,
    conv_one_bias,
    conv_two,
    conv_two_bias,
    lang_table,
    ln_one_gain,
    ln_one_bias,
    w_qkv,
    q_bias,
    v_bias,
    w_out,
    out_bias,
    ln_two_gain,
    ln_two_bias,
    w_fc_one,
    fc_one_bias,
    w_fc_two,
    fc_two_bias,
    grad_out,
):
    slots, part, width = grad_out.shape
    hidden = w_fc_one.shape[1]
    pairs = width // PAIR
    quarter = width // 4
    mels = mel.shape[2]
    rows = slots * part
    j = lax.axis_index("chan")
    x, c = j // 2, j % 2
    live = (x < clip_count[lax.axis_index("dp")]).astype(F32)

    def to_clip(block):
        same = send(pick(block, c, 0), SAME)
        other = send(pick(block, 1 - c, 0), OTHER)
        return ordered(x == 0, same, other)

    def send_back(block):
        half = block.shape[0] // 2
        first, second = block[:half], block[half:]
        same = send(jnp.where(x == 0, first, second), SAME_BACK)
        return same, send(jnp.where(x == 0, second, first), OTHER_BACK)

    def take_back(same, other):
        return ordered(c == 0, same, other, stack=True)

    mel_pairs = mel.reshape(slots, part, 2 * mels)
    edge = send(jnp.where(j == 1, mel_pairs[1, -1], mel_pairs[0, 0]), [(1, 3), (2, 0)])
    edge = jnp.where(j == 1, mel_pairs[0, -1], jnp.where(j == 2, mel_pairs[1, 0], edge))
    zero_edge = jnp.zeros_like(edge)
    mel_own = jnp.concatenate(
        [
            jnp.where(c == 1, edge, zero_edge)[None],
            to_clip(mel_pairs),
            jnp.where(c == 0, edge, zero_edge)[None],
        ]
    )

    y = lax.axis_index("dp") % 2
    index = jnp.stack([j, y])
    one_part = jnp.concatenate([conv_one.T, conv_one_bias[:, None]], axis=1)
    blocks = hidden // width
    up_part = jnp.stack(
        [w_out] + [w_fc_one[:, k * width : (k + 1) * width] for k in range(blocks)]
    )
    one_across = send(one_part, CROSS)
    qkv_part, down_part = w_qkv[None], w_fc_two[None]
    two_across = send(conv_two, CROSS)
    one_across, up_part, two_across = join(one_across, up_part, two_across)
    one_column = ordered(x == 0, one_part, one_across, stack=True)
    one_whole = ordered(c == 0, one_column, send(one_column, CORE), 1, stack=True)
    one_whole = one_whole.reshape(width, -1)

    def cross_half(own, side=y):
        half = own.shape[1] // 2
        return send(lax.dynamic_slice_in_dim(own, side * half, half, 1), CROSS)

    def cross_rest(far):
        return over_dp(far, 1)

    def beside(far, rest):
        return send(jnp.stack([far, rest]), CORE)

    two_near = send(conv_two, CORE)
    qkv_far = cross_half(after(qkv_part, two_across))

    mel_own, one_whole, qkv_far = join(mel_own, one_whole, qkv_far)
    two_beside = send(two_across, CORE)
    qkv_rest = cross_half(after(qkv_part, qkv_far), 1 - y)
    even, odd = mel_own[:, :mels], mel_own[:, mels:]
    ones = jnp.ones((rows, 1), BF16)
    cols_even = jnp.concatenate([odd[0:rows], even[1 : rows + 1], odd[1 : rows + 1], ones], axis=1)
    cols_odd = jnp.concatenate(
        [even[1 : rows + 1], odd[1 : rows + 1], even[2 : rows + 2], ones], axis=1
    )
    cols_edge = jnp.concatenate([even[0:1], odd[0:1], even[1:2], ones[0:1]], axis=1)
    hid_even, slope_even = gelu_both(mm_nt(cols_even, one_whole))
    hid_odd, slope_odd = gelu_both(mm_nt(cols_odd, one_whole))
    hid_edge, _ = gelu_both(mm_nt(cols_edge, one_whole))
    hid_edge = jnp.where(c == 1, hid_edge, 0.0)
    hid_even, hid_odd, hid_edge = hid_even.astype(BF16), hid_odd.astype(BF16), hid_edge.astype(BF16)
    slope_even, slope_odd = slope_even.astype(BF16), slope_odd.astype(BF16)
    hid_even, hid_odd, hid_edge, slope_even, slope_odd, two_beside = join(
        hid_even, hid_odd, hid_edge, slope_even, slope_odd, two_beside
    )
    hid_prev = jnp.concatenate([hid_edge, hid_odd[:-1]])
    hid_taps = jnp.concatenate([hid_prev, hid_even, hid_odd], axis=1)
    group = pick(lang_group, x, 0)
    place_rows = positions(rows, width, after(c * rows, hid_edge))
    place_rows += pick(lang_table, group, 0).astype(F32)[None]
    place_rows, hid_taps, qkv_rest = join(place_rows, hid_taps, qkv_rest)
    qkv_near = send(after(qkv_part, qkv_rest), CORE)
    qkv_beside = beside(qkv_far, qkv_rest)
    (two_full,) = place(
        index, (conv_two, two_near, two_across, two_beside), TAP_MOVES, (3, width, width)
    )
    two_full = two_full.reshape(-1, width)
    stem_act, slope_two = gelu_both(mm(hid_taps, two_full) + conv_two_bias.astype(F32))
    slope_two = slope_two.astype(BF16)
    stem = stem_act + place_rows

    gain_one, gain_two = ln_one_gain.astype(F32), ln_two_gain.astype(F32)
    stats_one = norm_stats(stem)
    normed = (
        (stem - stats_one[0]) * stats_one[1] * gain_one + ln_one_bias.astype(F32)
    ).astype(BF16)
    normed, slope_two, qkv_near, qkv_beside = join(normed, slope_two, qkv_near, qkv_beside)
    up_far = cross_half(after(up_part, qkv_rest))
    (qkv_full,) = place(
        index, (qkv_part, qkv_near, qkv_far, qkv_rest, qkv_beside), ROW_MOVES, (width, 3 * width)
    )
    kv_shift = jnp.concatenate([jnp.zeros((width,), F32), v_bias.astype(F32)])
    kv_own = (mm(normed, qkv_full[:, width:]) + kv_shift).astype(BF16)
    kv_oth = send(kv_own, CORE)
    queries = (mm(normed, qkv_full[:, :width]) + q_bias.astype(F32)).astype(BF16)
    queries, kv_oth = join(queries, kv_oth)
    half = pairs // 2
    partial = attend(queries, kv_own, kv_oth, 0, half, pairs)
    *partial, up_far = join(*partial, up_far)
    up_near = send(after(up_part, up_far), CORE)
    up_rest = cross_rest(up_far)
    down_far = cross_half(after(down_part, up_far))
    down_near = send(after(down_part, up_far), CORE)
    attended, lse = attend(queries, kv_own, kv_oth, half, pairs - half, pairs, partial)
    attended, up_near, up_rest, down_far, down_near = join(
        attended, up_near, up_rest, down_far, down_near
    )
    up_beside = beside(up_far, up_rest)
    down_rest = cross_rest(down_far)
    grad_part = after(grad_out, down_far)
    grad_same = send(pick(grad_part, c, 0), SAME)
    grad_other = send(pick(grad_part, 1 - c, 0), OTHER)
    out_full, up_full = place(
        index,
        (up_part, up_near, up_far, up_rest, up_beside),
        block_moves(blocks, width),
        (width, width),
        (width, hidden),
    )
    residual = stem + mm(attended, out_full) + out_bias.astype(F32)

    stats_two = norm_stats(residual)
    normed_two = (
        (residual - stats_two[0]) * stats_two[1] * gain_two + ln_two_bias.astype(F32)
    ).astype(BF16)
    active, slope_up = gelu_both(mm(normed_two, up_full) + fc_one_bias.astype(F32))
    active, slope_up = active.astype(BF16), slope_up.astype(BF16)

    def owner_terms(grads):
        return Terms(grads.astype(BF16).reshape(2, 2, -1, grads.shape[1]), ["x", "core"])

    def core_hop(terms):
        terms.hop("core", c, lambda block: send(block, CORE))

    def x_hop(terms):
        terms.hop("x", x, lambda block: send(block, CROSS))

    def first_hops(sides):
        x_hop(sides[0])
        sides[1].dp_hop(1)

    def second_hops(sides):
        sides[0].dp_hop(1)
        x_hop(sides[1])

    active, slope_up, down_rest, grad_same, grad_other = join(
        active, slope_up, down_rest, grad_same, grad_other
    )
    cotangent = ordered(x == 0, grad_same, grad_other)
    down_parts = (down_part, down_near, down_far, down_rest, beside(down_far, down_rest))
    (down_full,) = place(index, down_parts, ROW_MOVES, (hidden, width))
    grad_mlp = (cotangent.astype(F32) * live).astype(BF16)
    grad_rows = grad_mlp.astype(F32)
    down = owner_terms(mm_tn(active, grad_mlp))
    down_shift = jnp.sum(grad_rows, axis=0)
    grad_mlp = tie([down], grad_mlp)
    core_hop(down)
    grad_upper = (mm_nt(grad_mlp, down_full) * slope_up.astype(F32)).astype(BF16)
    up_shift = jnp.sum(grad_upper.astype(F32), axis=0)
    grad_upper = tie([down], grad_upper)
    x_hop(down)
    up = owner_terms(mm_tn(normed_two, grad_upper))
    grad_upper = tie([up], grad_upper)
    core_hop(up)
    grad_norm, grad_gain_two, grad_shift_two = norm_back(
        residual, stats_two, gain_two, mm_nt(grad_upper, up_full)
    )
    grad_residual = grad_rows + grad_norm
    grad_branch = grad_residual.astype(BF16)
    out_shift = jnp.sum(grad_branch.astype(F32), axis=0)
    out_grads = mm_tn(attended, grad_branch).astype(BF16)
    grad_att = mm_nt(grad_branch, out_full).astype(BF16)
    grad_att, out_grads = tie([up], grad_att, out_grads)

    third = -(-pairs // 3)
    operands = (queries, kv_own, kv_oth, lse)
    bits = dp_bits()
    partial = attend_back(*operands, grad_att, 0, third, pairs)
    partial = tie([down, up], *partial)
    x_hop(up)
    partial = attend_back(*operands, grad_att, third, third, pairs, partial)
    grad_q, own_kv, oth_kv = attend_back(
        *operands, grad_att, 2 * third, pairs - 2 * third, pairs, partial
    )
    grad_q, own_kv, oth_kv = tie([up], grad_q, own_kv, oth_kv)
    oth_kv = send(oth_kv, CORE)
    up_share = up.total()
    ffn = jnp.concatenate(
        [down.total()] + [up_share[:, k * width : (k + 1) * width] for k in range(blocks)]
    )
    ffn = Terms(ffn.reshape((2,) * len(bits) + (-1, width)), bits)
    ffn.dp_hop(1)
    encoded = (residual + mm(after(active, grad_q), down_full) + fc_two_bias.astype(F32)) * live
    encoded, own_kv, oth_kv = join(encoded.astype(BF16), own_kv, oth_kv)
    q_shift = jnp.sum(grad_q.astype(F32), axis=0)
    grad_kv = round_sum(own_kv, oth_kv)
    grad_packed = jnp.concatenate([grad_q, grad_kv[0], grad_kv[1]], axis=1)
    qkv_grads = jnp.concatenate([mm_tn(normed, grad_packed).astype(BF16), out_grads], axis=1)
    v_shift = jnp.sum(grad_kv[1].astype(F32), axis=0)
    qkv = owner_terms(qkv_grads)
    grad_packed = tie([qkv], grad_packed)
    core_hop(qkv)
    encoded = send_back(encoded)
    grad_normed = tie([qkv], mm_nt(grad_packed, qkv_full))

    def split_rows(terms):
        middle = terms.arrays[0].shape[-1] // 2
        sides = []
        for cut in (slice(0, middle), slice(middle, None)):
            side = Terms(None, ())
            side.terms = []
            for array, names in terms.terms:
                part = array[..., cut]
                shape = part.shape[: len(names)] + (2,) * len(bits)
                part = part.reshape(shape + (part.shape[-2] // 2 ** len(bits), middle))
                side.terms.append((part, names + tuple(bits)))
            side.fixed = dict(terms.fixed)
            sides.append(side)
        return sides

    qkv = split_rows(qkv)
    first_hops(qkv)
    grad_norm, grad_gain_one, grad_shift_one = norm_back(stem, stats_one, gain_one, grad_normed)
    grad_stem = grad_residual + grad_norm
    group_hot = (jnp.arange(lang_table.shape[0]) == group).astype(F32)
    grad_lang = group_hot[:, None] * jnp.sum(grad_stem, axis=0)[None]
    grad_two = (grad_stem * slope_two.astype(F32)).astype(BF16)
    two_shift = jnp.sum(grad_two.astype(F32), axis=0)
    two_grads = mm_tn(hid_taps, grad_two).astype(BF16).reshape(3, 2, 2, quarter, width)
    two = Terms(
        two_grads.transpose(1, 2, 0, 3, 4).reshape(2, 2, 3 * quarter, width), ["x", "core"]
    )
    grad_two, encoded = tie([two, ffn], grad_two, encoded)
    encoded = take_back(*encoded)
    core_hop(two)
    for bit in bits[1:2]:
        ffn.dp_hop(bit)
    follow = send(grad_two[0:1], [(1, 0), (3, 2)])
    vectors = jnp.concatenate(
        [
            jnp.stack(
                [
                    q_shift, v_shift, grad_gain_one, grad_shift_one, two_shift,
                    down_shift, grad_gain_two, grad_shift_two, out_shift,
                ]
            ),
            up_shift.reshape(-1, width),
            grad_lang,
        ]
    )
    hid_grad_even = mm_nt(grad_two, two_full[width : 2 * width])
    grad_even = (hid_grad_even * slope_even.astype(F32)).astype(BF16)
    grad_even, grad_two, follow, vectors = tie([two, ffn], grad_even, grad_two, follow, vectors)
    two = split_rows(two)
    first_hops(two)
    for bit in bits[2:]:
        ffn.dp_hop(bit)
    vectors += send(vectors, CORE)
    hid_grad_last = mm_nt(grad_two, two_full[2 * width :])
    grad_next = jnp.concatenate([grad_two[1:], follow])
    hid_grad_odd = hid_grad_last + mm_nt(grad_next, two_full[:width])
    grad_odd = (hid_grad_odd * slope_odd.astype(F32)).astype(BF16)
    grad_odd, vectors = tie(qkv + [ffn], grad_odd, vectors)
    second_hops(qkv)
    backs = list(reversed(bits))
    ffn = Gather(ffn.total())
    ffn.hop((backs[0],))
    vectors += send(vectors, CROSS)
    one_grads = mm_tn(grad_even, cols_even) + mm_tn(grad_odd, cols_odd)
    spare = width // 3 - one_grads.shape[1]
    one = owner_terms(jnp.pad(one_grads, ((0, 0), (0, spare))))
    grad_even, grad_odd, vectors = tie([one] + two, grad_even, grad_odd, vectors)
    second_hops(two)
    core_hop(one)
    vectors += over_dp(vectors, 1)
    terms_even = mm(grad_even, one_whole)
    terms_odd = mm(grad_odd, one_whole)
    before, mid_e, late = (terms_even[:, k * mels : (k + 1) * mels] for k in range(3))
    early, mid_o, last = (terms_odd[:, k * mels : (k + 1) * mels] for k in range(3))
    spill = send(jnp.where(c == 0, last[-1:], before[0:1]), CORE)
    zero_spill = jnp.zeros_like(spill)
    last_prev = jnp.concatenate([jnp.where(c == 1, spill, zero_spill), last[:-1]])
    before_next = jnp.concatenate([before[1:], jnp.where(c == 0, spill, zero_spill)])
    mel_grad = jnp.concatenate(
        [mid_e + early + last_prev, late + mid_o + before_next], axis=1
    ).astype(BF16)
    mel_grad, vectors = tie([one, ffn] + qkv, mel_grad, vectors)
    x_hop(one)
    for bit in backs[1:-1]:
        ffn.hop((bit,))
    for side in qkv:
        side.terms, side.fixed = [(side.total(), tuple(bits[1:]))], {}
    qkv = Terms(jnp.stack([side.arrays[0] for side in qkv], axis=len(bits) - 1), bits[1:])
    qkv.rest_hops()
    mel_grad, vectors = tie([one], mel_grad, vectors)
    one_share = one.total()
    one_rows = one_share.shape[0] // 3
    flat = jnp.concatenate([one_share[k * one_rows : (k + 1) * one_rows] for k in range(3)], axis=1)
    flat = Terms(
        jnp.stack([flat[:, : width // 2], flat[:, width // 2 :]]).swapaxes(0, 1).reshape(
            (2,) * len(bits) + (one_rows // 2 ** len(bits), 2, width // 2)
        ).swapaxes(-3, -2),
        bits,
    )
    flat.dp_hop(1)
    mel_grad = send_back(mel_grad)
    mel_grad, vectors = tie([flat, ffn] + two, mel_grad, vectors)
    conv = jnp.stack([side.total() for side in two], axis=len(bits) - 1)
    conv = Terms(jnp.concatenate([conv, flat.total()], axis=-2), bits[1:])
    conv.rest_hops()
    ffn.hop((1,))
    vectors = tie([qkv, conv], vectors)
    qkv = Gather(qkv.total(), 1)
    qkv.rest_hops()
    conv = Gather(conv.total(), 1)
    conv.rest_hops()
    for bit in bits[1:2]:
        vectors += over_dp(vectors, bit)
    mel_grad = take_back(*mel_grad).astype(F32).reshape(slots, 2 * part, mels)
    mel_grad, vectors = tie([qkv, conv, ffn], mel_grad, vectors)
    qkv.hop((1,))
    conv.hop((1,))
    for bit in bits[2:]:
        vectors += over_dp(vectors, bit)
    tie([qkv])
    qkv_share = qkv.settle()
    vectors = tie([conv], vectors)
    conv = conv.settle()
    ffn = ffn.settle().astype(F32)
    down_sum = ffn[: hidden // 4]
    up_sum = jnp.concatenate(
        [ffn[hidden // 4 + k * quarter : hidden // 4 + (k + 1) * quarter] for k in range(blocks)],
        axis=1,
    )

    def columns(sides):
        return jnp.concatenate([sides[0], sides[1]], axis=1).astype(F32)

    qkv_out = columns(qkv_share)
    pieces = 2 ** len(bits)
    conv_pieces = columns(conv).reshape(pieces, -1, width)
    taken = 3 * quarter // pieces
    two_sum = conv_pieces[:, :taken].reshape(conv_two.shape)
    one_flat = conv_pieces[:, taken:].reshape(one_rows, width)
    one_sum = jnp.concatenate(
        [one_flat[:, k * width // 3 : (k + 1) * width // 3] for k in range(3)]
    )
    vec = lambda k: vectors[k]
    return (
        encoded,
        mel_grad,
        one_sum[:, : 3 * mels].T,
        one_sum[:, 3 * mels],
        two_sum,
        vec(4),
        vectors[9 + blocks :],
        vec(2),
        vec(3),
        qkv_out[:, : 3 * width],
        vec(0),
        vec(1),
        qkv_out[:, 3 * width :],
        vec(8),
        vec(6),
        vec(7),
        up_sum,
        vectors[9 : 9 + blocks].reshape(-1),
        down_sum,
        vec(5),
    )


def solution(mesh):
    in_specs = (
        P("dp", "chan", None),
        P("dp"),
        P(),
        P(None, "chan"),
        P("chan"),
        P(None, "chan", None),
        P(),
        P(),
        P(),
        P(),
        P("chan", None),
        P(),
        P(),
        P("chan", None),
        P(),
        P(),
        P(),
        P("chan", None),
        P(),
        P("chan", None),
        P(),
        P("dp", "chan", None),
    )
    out_specs = (
        P("dp", "chan", None),
        P("dp", "chan", None),
        P(None, "chan"),
        P("chan"),
        P(None, "chan", None),
        P(),
        P(),
        P(),
        P(),
        P("chan", None),
        P(),
        P(),
        P("chan", None),
        P(),
        P(),
        P(),
        P("chan", None),
        P(),
        P("chan", None),
        P(),
    )
    return jax.shard_map(
        on_device, mesh=mesh, in_specs=in_specs, out_specs=out_specs, check_vma=False
    )
```

profile of v0, /device:TPU:0, one launch (start us, length us, event | category | flops | bytes accessed | tf_op | source)
XLA Modules:
  0.0 443.0 jit_solution(6201753264681985807)
XLA Ops:
  34.8 7.4 %collective-permute-done.6.refs_3_ = bf16[1,96,2304]{2,1,0:T(8,128)(2,1)S(1)} collective-permute-done((bf16[1,96,2304]{2,1,0:T(8,128)(2,1)S(1)}, bf16[1,96,2304]{2,1,0:T(8,128)(2,1)S(1)}, u32[]{:S(2)}, u32[]{:S(2)}) %collective-permute-start.6) | collective-permute-done | bytes 442400 | tf_op jit(solution)/shard_map/ppermute | solution.py:25
  49.1 3.8 multiply_sine_fusion
  73.0 11.2 %attend.2 = (bf16[704,768]{1,0:T(8,128)(2,1)}, f32[704,768]{1,0:T(8,128)}) custom-call(bf16[704,768]{1,0:T(8,128)(2,1)} %add_convert_fusion.3.refs_0_, bf16[704,1536]{1,0:T(8,128)(2,1)} %copy-done.17, bf16[704,1536]{1,0:T(8,128)(2,1)} %copy-done.18, bf16[704,1536]{1,0:T(8,128)(2,1)} %copy-done.17, bf16[704,1536]{1,0:T(8,128)(2,1)} %copy-done.18), custom_call_target="tpu_custom_call" | custom-call | flops 3045064704 | bytes 4325376 | tf_op jit(solution)/shard_map/attend/pallas_call | solution.py:116
  91.0 11.0 %attend.3 = (bf16[704,768]{1,0:T(8,128)(2,1)}, f32[704,768]{1,0:T(8,128)}) custom-call(bf16[704,768]{1,0:T(8,128)(2,1)} %add_convert_fusion.3.refs_0_, bf16[704,1536]{1,0:T(8,128)(2,1)} %copy-done.17, bf16[704,1536]{1,0:T(8,128)(2,1)} %copy-done.18, bf16[704,1536]{1,0:T(8,128)(2,1)} %copy-done.17, ...), custom_call_target="tpu_custom_call", output_to_operand_aliasing={{0}: (5, {}), {1}: (6, {})} | custom-call | flops 3045064704 | bytes 4325376 | tf_op jit(solution)/shard_map/attend/pallas_call | solution.py:116
  124.5 8.8 %fusion.4 = (bf16[704,3072]{1,0:T(8,128)(2,1)}, bf16[704,3072]{1,0:T(8,128)(2,1)S(1)}) fusion(f32[3072]{0:T(1024)S(1)} %copy-done.83, bf16[768,3072]{1,0:T(8,128)(2,1)S(1)} %get-tuple-element.243, f32[704,768]{1,0:T(8,128)S(1)} %get-tuple-element.526, f32[768]{0:T(1024)S(1)} %copy-done.87, f32[768]{0:T(1024)S(1)} %copy-done.82, f32[704]{0:T(1024)S(1)} %add_rsqrt_fusion, ...), kind=kOutput, calls=%fused_computation.5 | convolution fusion | flops 3350544384 | bytes 15556096 | tf_op jit(solution)/shard_map/dot_general | solution.py:68
  134.9 4.3 convolution_convert_fusion.3
  142.0 5.1 %collective-permute-done.23.refs_5_ = bf16[2,1,384,768]{3,2,1,0:T(8,128)(2,1)S(1)} collective-permute-done((bf16[2,1,384,768]{3,2,1,0:T(8,128)(2,1)S(1)}, bf16[2,1,384,768]{3,2,1,0:T(8,128)(2,1)S(1)}, u32[]{:S(2)}, u32[]{:S(2)}) %collective-permute-start.23) | collective-permute-done | bytes 1179680 | tf_op jit(solution)/shard_map/ppermute | solution.py:25
  151.4 3.8 convert_reduce_fusion
  155.3 5.0 %convolution_convert_fusion.2 = bf16[768,3072]{1,0:T(8,128)(2,1)S(1)} fusion(bf16[704,3072]{1,0:T(8,128)(2,1)S(1)} %get-tuple-element.255, f32[704,768]{1,0:T(8,128)S(1)} %copy-done.20, f32[768]{0:T(1024)S(1)} %copy-done.87, f32[768]{0:T(1024)S(1)} %copy-done.82, f32[704]{0:T(1024)S(1)} %add_rsqrt_fusion, f32[704]{0:T(1024)S(1)} %broadcast_multiply_fusion.5), kind=kOutput, calls=%fused_computation.12 | convolution fusion | flops 3326951424 | bytes 11218432 | tf_op jit(solution)/shard_map/dot_general | solution.py:76
  160.7 4.2 fusion.12
  165.0 4.0 multiply_reduce_fusion
  174.9 14.2 %attend_back.3 = (bf16[704,768]{1,0:T(8,128)(2,1)}, bf16[2,704,768]{2,1,0:T(8,128)(2,1)}, bf16[2,704,768]{2,1,0:T(8,128)(2,1)}) custom-call(bf16[704,768]{1,0:T(8,128)(2,1)} %add_convert_fusion.3.refs_0_, bf16[704,1536]{1,0:T(8,128)(2,1)} %copy-done.17, bf16[704,1536]{1,0:T(8,128)(2,1)} %copy-done.18, bf16[704,1536]{1,0:T(8,128)(2,1)} %copy-done.17, ...), custom_call_target="tpu_custom_call" | custom-call | flops 5075107840 | bytes 4685824 | tf_op jit(solution)/shard_map/attend_back/pallas_call | solution.py:178
  189.1 4.1 collective-permute-done.24
  196.2 13.8 %attend_back.4 = (bf16[704,768]{1,0:T(8,128)(2,1)}, bf16[2,704,768]{2,1,0:T(8,128)(2,1)}, bf16[2,704,768]{2,1,0:T(8,128)(2,1)}) custom-call(bf16[704,768]{1,0:T(8,128)(2,1)} %add_convert_fusion.3.refs_0_, bf16[704,1536]{1,0:T(8,128)(2,1)} %copy-done.17, bf16[704,1536]{1,0:T(8,128)(2,1)} %copy-done.18, ...), custom_call_target="tpu_custom_call", output_to_operand_aliasing={{0}: (7, {}), {1}: (8, {}), {2}: (9, {})} | custom-call | flops 5075107840 | bytes 4685824 | tf_op jit(solution)/shard_map/attend_back/pallas_call | solution.py:178
  210.1 13.8 %attend_back.5 = (bf16[704,768]{1,0:T(8,128)(2,1)}, bf16[2,704,768]{2,1,0:T(8,128)(2,1)}, bf16[2,704,768]{2,1,0:T(8,128)(2,1)}) custom-call(bf16[704,768]{1,0:T(8,128)(2,1)} %add_convert_fusion.3.refs_0_, bf16[704,1536]{1,0:T(8,128)(2,1)} %copy-done.17, bf16[704,1536]{1,0:T(8,128)(2,1)} %copy-done.18, ...), custom_call_target="tpu_custom_call", output_to_operand_aliasing={{0}: (7, {}), {1}: (8, {}), {2}: (9, {})} | custom-call | flops 5075107840 | bytes 4685824 | tf_op jit(solution)/shard_map/attend_back/pallas_call | solution.py:178
  233.0 8.3 %multiply_convert_fusion.5 = bf16[704,768]{1,0:T(8,128)(2,1)} fusion(f32[704,768]{1,0:T(8,128)S(1)} %copy-done.20, bf16[704,3072]{1,0:T(8,128)(2,1)} %copy-done.101, bf16[3072,768]{1,0:T(8,128)(2,1)} %copy-done, f32[768]{0:T(1024)S(1)} %convert_element_type.701, f32[]{:T(128)S(6)} %convert_element_type.681), kind=kOutput, calls=%fused_computation.68 | convolution fusion | flops 3324051456 | bytes 12291076 | tf_op jit(solution)/shard_map/dot_general | solution.py:68
  246.0 4.0 convolution_convert_fusion.1
  269.5 10.8 %collective-permute-done.29 = bf16[2,2,192,768]{3,2,1,0:T(8,128)(2,1)S(1)} collective-permute-done((bf16[2,2,192,768]{3,2,1,0:T(8,128)(2,1)S(1)}, bf16[2,2,192,768]{3,2,1,0:T(8,128)(2,1)S(1)}, u32[]{:S(2)}, u32[]{:S(2)}) %collective-permute-start.29) | collective-permute-done | bytes 1179680 | tf_op jit(solution)/shard_map/ppermute | solution.py:280
  295.8 4.4 concatenate.195
  343.3 4.2 collective-permute-done.43
  374.8 8.3 %collective-permute-done.58 = bf16[2,80,384]{2,1,0:T(8,128)(2,1)S(1)} collective-permute-done((bf16[2,80,384]{2,1,0:T(8,128)(2,1)S(1)}, bf16[2,80,384]{2,1,0:T(8,128)(2,1)S(1)}, u32[]{:S(2)}, u32[]{:S(2)}) %collective-permute-start.58) | collective-permute-done | bytes 122912 | tf_op jit(solution)/shard_map/ppermute | solution.py:392
  389.8 8.1 %collective-permute-done.68 = f32[29,768]{1,0:T(8,128)S(1)} collective-permute-done((f32[29,768]{1,0:T(8,128)S(1)}, f32[29,768]{1,0:T(8,128)S(1)}, u32[]{:S(2)}, u32[]{:S(2)}) %collective-permute-start.68) | collective-permute-done | bytes 89120 | tf_op jit(solution)/shard_map/ppermute | solution.py:280
  424.4 5.4 %collective-permute-done.69 = bf16[2,320,384]{2,1,0:T(8,128)(2,1)} collective-permute-done((bf16[2,320,384]{2,1,0:T(8,128)(2,1)S(1)}, bf16[2,320,384]{2,1,0:T(8,128)(2,1)}, u32[]{:S(2)}, u32[]{:S(2)}) %collective-permute-start.69) | collective-permute-done | bytes 491552 | tf_op jit(solution)/shard_map/ppermute | solution.py:280
  436.1 3.7 collective-permute-done.71
  (555 shorter events, 265.5 us)
Async XLA Ops:
  0.7 31.4 %collective-permute-start.4 = (bf16[3,192,768]{2,1,0:T(8,128)(2,1)}, bf16[3,192,768]{2,1,0:T(8,128)(2,1)S(1)}, u32[]{:S(2)}, u32[]{:S(2)}) collective-permute-start(bf16[3,192,768]{2,1,0:T(8,128)(2,1)} %refs_1_.1), channel_id=1, source_target_pairs={{0,2},{1,3},{2,0},{3,1},{4,6},{5,7},{6,4},{7,5},{8,10},{9,11},{10,... | collective-permute-start | bytes 2654216 | tf_op jit(solution)/shard_map/ppermute | solution.py:25
  3.7 50.7 %collective-permute-start.9 = (bf16[3,192,768]{2,1,0:T(8,128)(2,1)}, bf16[3,192,768]{2,1,0:T(8,128)(2,1)}, u32[]{:S(2)}, u32[]{:S(2)}) collective-permute-start(bf16[3,192,768]{2,1,0:T(8,128)(2,1)} %refs_1_.1), channel_id=1, source_target_pairs={{0,1},{1,0},{2,3},{3,2},{4,5},{5,4},{6,7},{7,6},{8,9},{9,8},{10,11... | collective-permute-start | bytes 2654216 | tf_op jit(solution)/shard_map/ppermute | solution.py:25
  5.8 23.1 %collective-permute-start.1 = (bf16[352,160]{1,0:T(8,128)(2,1)}, bf16[352,160]{1,0:T(8,128)(2,1)}, u32[]{:S(2)}, u32[]{:S(2)}) collective-permute-start(bf16[352,160]{1,0:T(8,128)(2,1)} %get-tuple-element.509), channel_id=1, source_target_pairs={{0,0},{1,2},{2,1},{3,3},{4,4},{5,6},{6,5},{7,7},{8,8},{9,10},{10,9... | collective-permute-start | bytes 337928 | tf_op jit(solution)/shard_map/ppermute | solution.py:25
  8.8 20.2 %collective-permute-start.2 = (bf16[352,160]{1,0:T(8,128)(2,1)}, bf16[352,160]{1,0:T(8,128)(2,1)}, u32[]{:S(2)}, u32[]{:S(2)}) collective-permute-start(bf16[352,160]{1,0:T(8,128)(2,1)} %get-tuple-element.510), channel_id=1, source_target_pairs={{0,2},{1,0},{2,3},{3,1},{4,6},{5,4},{6,7},{7,5},{8,10},{9,8},{10,1... | collective-permute-start | bytes 337928 | tf_op jit(solution)/shard_map/ppermute | solution.py:25
  68.5 19.0 %collective-permute-start.13 = (bf16[5,96,768]{2,1,0:T(8,128)(2,1)}, bf16[5,96,768]{2,1,0:T(8,128)(2,1)S(1)}, u32[]{:S(2)}, u32[]{:S(2)}) collective-permute-start(bf16[5,96,768]{2,1,0:T(8,128)(2,1)} %constant_dynamic-slice_fusion.1), channel_id=1, source_target_pairs={{0,2},{1,3},{2,0},{3,1},{4,6},{5,7},{6,4},{7,5},{8,10},{9,11},{10,... | collective-permute-start | bytes 2211848 | tf_op jit(solution)/shard_map/ppermute | solution.py:25
  87.4 18.9 %collective-permute-start.14 = (bf16[5,192,768]{2,1,0:T(8,128)(2,1)S(1)}, bf16[5,192,768]{2,1,0:T(8,128)(2,1)}, u32[]{:S(2)}, u32[]{:S(2)}) collective-permute-start(bf16[5,192,768]{2,1,0:T(8,128)(2,1)S(1)} %bitcast_dynamic-update-slice_fusion.refs_1_), channel_id=1, source_target_pairs={{0,1},{1,0},{2,3},{3,2},{4,5},{5,4},{6,7},{7,6},{8,9},{9,8},{10,11... | collective-permute-start | bytes 4423688 | tf_op jit(solution)/shard_map/ppermute | solution.py:25
  87.4 18.9 %collective-permute-start.17 = (bf16[1,768,768]{2,1,0:T(8,128)(2,1)}, bf16[1,768,768]{2,1,0:T(8,128)(2,1)}, u32[]{:S(2)}, u32[]{:S(2)}) collective-permute-start(bf16[1,768,768]{2,1,0:T(8,128)(2,1)} %bitcast.21.refs_1_), channel_id=1, source_target_pairs={{0,1},{1,0},{2,3},{3,2},{4,5},{5,4},{6,7},{7,6},{8,9},{9,8},{10,11... | collective-permute-start | bytes 3538952 | tf_op jit(solution)/shard_map/ppermute | solution.py:25
  88.0 18.4 %collective-permute-start.15 = (bf16[5,96,768]{2,1,0:T(8,128)(2,1)S(1)}, bf16[5,96,768]{2,1,0:T(8,128)(2,1)S(1)}, u32[]{:S(2)}, u32[]{:S(2)}) collective-permute-start(bf16[5,96,768]{2,1,0:T(8,128)(2,1)S(1)} %collective-permute-done.13.refs_3_), channel_id=1, source_target_pairs={{0,4},{4,0},{8,12},{12,8},{16,20},{20,16},{24,28},{28,24},{1,5},{5... | collective-permute-start | bytes 2211848 | tf_op jit(solution)/shard_map/ppermute | solution.py:280
  111.9 21.4 %collective-permute-start.19 = (bf16[1,384,768]{2,1,0:T(8,128)(2,1)S(1)}, bf16[1,384,768]{2,1,0:T(8,128)(2,1)S(1)}, u32[]{:S(2)}, u32[]{:S(2)}) collective-permute-start(bf16[1,384,768]{2,1,0:T(8,128)(2,1)S(1)} %collective-permute-done.16.refs_3_), channel_id=1, source_target_pairs={{0,4},{4,0},{8,12},{12,8},{16,20},{20,16},{24,28},{28,24},{1,5},{5... | collective-permute-start | bytes 1769480 | tf_op jit(solution)/shard_map/ppermute | solution.py:280
  114.8 18.6 %collective-permute-start.20 = (bf16[352,768]{1,0:T(8,128)(2,1)S(1)}, bf16[352,768]{1,0:T(8,128)(2,1)S(1)}, u32[]{:S(2)}, u32[]{:S(2)}) collective-permute-start(bf16[352,768]{1,0:T(8,128)(2,1)S(1)} %get-tuple-element.496), channel_id=1, source_target_pairs={{0,0},{1,2},{2,1},{3,3},{4,4},{5,6},{6,5},{7,7},{8,8},{9,10},{10,9... | collective-permute-start | bytes 1622024 | tf_op jit(solution)/shard_map/ppermute | solution.py:25
  115.5 17.8 %collective-permute-start.21 = (bf16[352,768]{1,0:T(8,128)(2,1)S(1)}, bf16[352,768]{1,0:T(8,128)(2,1)S(1)}, u32[]{:S(2)}, u32[]{:S(2)}) collective-permute-start(bf16[352,768]{1,0:T(8,128)(2,1)S(1)} %get-tuple-element.495), channel_id=1, source_target_pairs={{0,2},{1,0},{2,3},{3,1},{4,6},{5,4},{6,7},{7,5},{8,10},{9,8},{10,1... | collective-permute-start | bytes 1622024 | tf_op jit(solution)/shard_map/ppermute | solution.py:25
  164.9 28.3 %collective-permute-start.24 = (bf16[768,768]{1,0:T(8,128)(2,1)}, bf16[768,768]{1,0:T(8,128)(2,1)}, u32[]{:S(2)}, u32[]{:S(2)}) collective-permute-start(bf16[768,768]{1,0:T(8,128)(2,1)} %fusion.12), channel_id=1, source_target_pairs={{0,2},{1,3},{2,0},{3,1},{4,6},{5,7},{6,4},{7,5},{8,10},{9,11},{10,... | collective-permute-start | bytes 3538952 | tf_op jit(solution)/shard_map/ppermute | solution.py:25
  195.9 28.0 %collective-permute-start.26 = (bf16[192,3072]{1,0:T(8,128)(2,1)}, bf16[192,3072]{1,0:T(8,128)(2,1)}, u32[]{:S(2)}, u32[]{:S(2)}) collective-permute-start(bf16[192,3072]{1,0:T(8,128)(2,1)} %fusion.11), channel_id=1, source_target_pairs={{0,2},{1,3},{2,0},{3,1},{4,6},{5,7},{6,4},{7,5},{8,10},{9,11},{10,... | collective-permute-start | bytes 3538952 | tf_op jit(solution)/shard_map/ppermute | solution.py:25
  252.4 28.0 %collective-permute-start.29 = (bf16[2,2,192,768]{3,2,1,0:T(8,128)(2,1)S(1)}, bf16[2,2,192,768]{3,2,1,0:T(8,128)(2,1)S(1)}, u32[]{:S(2)}, u32[]{:S(2)}) collective-permute-start(bf16[2,2,192,768]{3,2,1,0:T(8,128)(2,1)S(1)} %dynamic-slice_bitcast_fusion.4), channel_id=1, source_target_pairs={{0,4},{4,0},{8,12},{12,8},{16,20},{20,16},{24,28},{28,24},{1,5},{5... | collective-permute-start | bytes 3538952 | tf_op jit(solution)/shard_map/ppermute | solution.py:280
  254.2 26.1 %collective-permute-start.30 = (bf16[352,768]{1,0:T(8,128)(2,1)S(1)}, bf16[352,768]{1,0:T(8,128)(2,1)S(1)}, u32[]{:S(2)}, u32[]{:S(2)}) collective-permute-start(bf16[352,768]{1,0:T(8,128)(2,1)S(1)} %get-tuple-element.494), channel_id=1, source_target_pairs={{0,0},{2,1},{1,2},{3,3},{4,4},{6,5},{5,6},{7,7},{8,8},{10,9},{9,10... | collective-permute-start | bytes 1622024 | tf_op jit(solution)/shard_map/ppermute | solution.py:25
  255.1 25.3 %collective-permute-start.31 = (bf16[352,768]{1,0:T(8,128)(2,1)S(1)}, bf16[352,768]{1,0:T(8,128)(2,1)S(1)}, u32[]{:S(2)}, u32[]{:S(2)}) collective-permute-start(bf16[352,768]{1,0:T(8,128)(2,1)S(1)} %get-tuple-element.493), channel_id=1, source_target_pairs={{2,0},{0,1},{3,2},{1,3},{6,4},{4,5},{7,6},{5,7},{10,8},{8,9},{11,1... | collective-permute-start | bytes 1622024 | tf_op jit(solution)/shard_map/ppermute | solution.py:25
  281.6 18.7 %collective-permute-start.33 = (bf16[2,192,768]{2,1,0:T(8,128)(2,1)}, bf16[2,192,768]{2,1,0:T(8,128)(2,1)}, u32[]{:S(2)}, u32[]{:S(2)}) collective-permute-start(bf16[2,192,768]{2,1,0:T(8,128)(2,1)} %fusion.35), channel_id=1, source_target_pairs={{0,8},{4,12},{8,0},{12,4},{16,24},{20,28},{24,16},{28,20},{1,9},{5... | collective-permute-start | bytes 1769480 | tf_op jit(solution)/shard_map/ppermute | solution.py:280
  288.7 30.3 %collective-permute-start.36 = (bf16[2,2,2,24,1536]{4,3,2,1,0:T(8,128)(2,1)}, bf16[2,2,2,24,1536]{4,3,2,1,0:T(8,128)(2,1)}, u32[]{:S(2)}, u32[]{:S(2)}) collective-permute-start(bf16[2,2,2,24,1536]{4,3,2,1,0:T(8,128)(2,1)} %fusion.33), channel_id=1, source_target_pairs={{0,4},{4,0},{8,12},{12,8},{16,20},{20,16},{24,28},{28,24},{1,5},{5... | collective-permute-start | bytes 1769480 | tf_op jit(solution)/shard_map/ppermute | solution.py:280
  290.2 28.8 %collective-permute-start.35 = (bf16[2,2,2,24,1536]{4,3,2,1,0:T(8,128)(2,1)}, bf16[2,2,2,24,1536]{4,3,2,1,0:T(8,128)(2,1)}, u32[]{:S(2)}, u32[]{:S(2)}) collective-permute-start(bf16[2,2,2,24,1536]{4,3,2,1,0:T(8,128)(2,1)} %fusion.34), channel_id=1, source_target_pairs={{0,2},{1,3},{2,0},{3,1},{4,6},{5,7},{6,4},{7,5},{8,10},{9,11},{10,... | collective-permute-start | bytes 1769480 | tf_op jit(solution)/shard_map/ppermute | solution.py:25
  312.9 20.9 %collective-permute-start.40 = (bf16[2,2,2,72,384]{4,3,2,1,0:T(8,128)(2,1)}, bf16[2,2,2,72,384]{4,3,2,1,0:T(8,128)(2,1)}, u32[]{:S(2)}, u32[]{:S(2)}) collective-permute-start(bf16[2,2,2,72,384]{4,3,2,1,0:T(8,128)(2,1)} %fusion.40), channel_id=1, source_target_pairs={{0,4},{4,0},{8,12},{12,8},{16,20},{20,16},{24,28},{28,24},{1,5},{5... | collective-permute-start | bytes 1327112 | tf_op jit(solution)/shard_map/ppermute | solution.py:280
  347.7 17.8 %collective-permute-start.53 = (bf16[384,768]{1,0:T(8,128)(2,1)S(1)}, bf16[384,768]{1,0:T(8,128)(2,1)S(1)}, u32[]{:S(2)}, u32[]{:S(2)}) collective-permute-start(bf16[384,768]{1,0:T(8,128)(2,1)S(1)} %maximum_select_fusion.6), channel_id=1, source_target_pairs={{0,8},{4,12},{8,0},{12,4},{16,24},{20,28},{24,16},{28,20},{1,9},{5... | collective-permute-start | bytes 1769480 | tf_op jit(solution)/shard_map/ppermute | solution.py:280
  372.9 36.0 %collective-permute-start.67 = (bf16[768,768]{1,0:T(8,128)(2,1)S(1)}, bf16[768,768]{1,0:T(8,128)(2,1)S(1)}, u32[]{:S(2)}, u32[]{:S(2)}) collective-permute-start(bf16[768,768]{1,0:T(8,128)(2,1)S(1)} %maximum_select_fusion.1), channel_id=1, source_target_pairs={{0,4},{4,0},{8,12},{12,8},{16,20},{20,16},{24,28},{28,24},{1,5},{5... | collective-permute-start | bytes 3538952 | tf_op jit(solution)/shard_map/ppermute | solution.py:280
  389.1 19.7 %collective-permute-start.61 = (bf16[2,24,1536]{2,1,0:T(8,128)(2,1)}, bf16[2,24,1536]{2,1,0:T(8,128)(2,1)}, u32[]{:S(2)}, u32[]{:S(2)}) collective-permute-start(bf16[2,24,1536]{2,1,0:T(8,128)(2,1)} %fusion.66), channel_id=1, source_target_pairs={{0,16},{4,20},{8,24},{12,28},{16,0},{20,4},{24,8},{28,12},{1,17},{... | collective-permute-start | bytes 442376 | tf_op jit(solution)/shard_map/ppermute | solution.py:392
  421.7 18.2 %collective-permute-start.71 = (bf16[2,96,1536]{2,1,0:T(8,128)(2,1)S(1)}, bf16[2,96,1536]{2,1,0:T(8,128)(2,1)S(1)}, u32[]{:S(2)}, u32[]{:S(2)}) collective-permute-start(bf16[2,96,1536]{2,1,0:T(8,128)(2,1)S(1)} %maximum_select_fusion.7), channel_id=1, source_target_pairs={{0,4},{4,0},{8,12},{12,8},{16,20},{20,16},{24,28},{28,24},{1,5},{5... | collective-permute-start | bytes 1769480 | tf_op jit(solution)/shard_map/ppermute | solution.py:280
  (152 other events, 1228.2 us)
where the time goes:
time: 448 us; the launch traced here: 443 us
  waiting for transfers between devices  81.5 us (18%)
  other arithmetic  78.3 us (17%)
  starting transfers between devices  78.2 us (17%)
  Pallas kernels  73.6 us (16%)
  matrix products  68 us (15%)
  local copies, waits for them, and re-layouts  57.8 us (13%)
  between operations  5.66 us (1%)
    pallas_call x3, Pallas kernels, attend_back(): pl.pallas_call(lambda *refs: attend_back_kernel(chunk, *refs), grid=(coun...  41.9 us
    ppermute x42, starting transfers between devices, send(): return lax.ppermute(block, 'chan', perm)  38.9 us
    ppermute x18, waiting for transfers between devices, over_dp(): lax.ppermute(block, 'dp', [(d, d ^ bit) for d in range(lax.axis_size('dp'...  38.8 us
    ppermute x42, waiting for transfers between devices, send(): return lax.ppermute(block, 'chan', perm)  30.7 us
    convert_element_type x20, other arithmetic, round_sum(): return sum((term.astype(F32) for term in terms)).astype(BF16)  27.2 us
    dot_general x8, matrix products, mm(): return jnp.dot(left, right, preferred_element_type=F32)  26.9 us
    ppermute x18, starting transfers between devices, over_dp(): lax.ppermute(block, 'dp', [(d, d ^ bit) for d in range(lax.axis_size('dp'...  23.1 us
    dot_general x10, matrix products, mm_nt(): lax.dot_general(left, right, (((1,), (1,)), ((), ())), preferred_element_...  22.2 us
  transfers between devices with their start and end apart: 72, of which 22 were waited for; matrix products, arithmetic and copies ran while one was open for 36% of the time, Pallas kernels for 16%

commit v1 on v0

--- a/solution.py
+++ b/solution.py
@@ -614,10 +614,7 @@
     partial = attend_back(*operands, grad_att, 0, third, pairs)
     partial = tie([down, up], *partial)
     x_hop(up)
-    partial = attend_back(*operands, grad_att, third, third, pairs, partial)
-    grad_q, own_kv, oth_kv = attend_back(
-        *operands, grad_att, 2 * third, pairs - 2 * third, pairs, partial
-    )
+    grad_q, own_kv, oth_kv = attend_back(*operands, grad_att, third, pairs - third, pairs, partial)
     grad_q, own_kv, oth_kv = tie([up], grad_q, own_kv, oth_kv)
     oth_kv = send(oth_kv, CORE)
     up_share = up.total()

time: 448 us -> 447 us (level)
  starting transfers between devices: 78.2 us -> 73.3 us
  waiting for transfers between devices: 81.5 us -> 86.2 us
    ppermute x42, starting transfers between devices: 38.9 us -> 33.2 us  [send(): return lax.ppermute(block, 'chan', perm)]
    pallas_call x3 -> x2, Pallas kernels: 41.9 us -> 39.6 us  [attend_back(): pl.pallas_call(lambda *refs: attend_back_kernel(chunk, *refs), grid=(coun...]
where the time goes in v1:
time: 447 us; the launch traced here: 442 us
  waiting for transfers between devices  86.2 us (19%)
  other arithmetic  78.3 us (18%)
  starting transfers between devices  73.3 us (16%)
  Pallas kernels  71.5 us (16%)
  matrix products  68.1 us (15%)
  local copies, waits for them, and re-layouts  59 us (13%)
  between operations  5.67 us (1%)
    ppermute x18, waiting for transfers between devices, over_dp(): lax.ppermute(block, 'dp', [(d, d ^ bit) for d in range(lax.axis_size('dp'...  43.1 us
    pallas_call x2, Pallas kernels, attend_back(): pl.pallas_call(lambda *refs: attend_back_kernel(chunk, *refs), grid=(coun...  39.6 us
    ppermute x42, starting transfers between devices, send(): return lax.ppermute(block, 'chan', perm)  33.2 us
    ppermute x42, waiting for transfers between devices, send(): return lax.ppermute(block, 'chan', perm)  33 us
    convert_element_type x20, other arithmetic, round_sum(): return sum((term.astype(F32) for term in terms)).astype(BF16)  27.1 us
    dot_general x8, matrix products, mm(): return jnp.dot(left, right, preferred_element_type=F32)  26.9 us
    ppermute x18, starting transfers between devices, over_dp(): lax.ppermute(block, 'dp', [(d, d ^ bit) for d in range(lax.axis_size('dp'...  23.9 us
    pallas_call x2, Pallas kernels, attend(): pl.pallas_call(lambda *refs: attend_kernel(chunk, *refs), grid=(count,),...  22.5 us
  transfers between devices with their start and end apart: 72, of which 22 were waited for; matrix products, arithmetic and copies ran while one was open for 36% of the time, Pallas kernels for 16%

profile of v1, /device:TPU:0, one launch (start us, length us, event | category | flops | bytes accessed | tf_op | source)
XLA Modules:
  0.0 442.1 jit_solution(7045193603834957354)
XLA Ops:
  34.7 7.7 %collective-permute-done.6.refs_3_ = bf16[1,96,2304]{2,1,0:T(8,128)(2,1)S(1)} collective-permute-done((bf16[1,96,2304]{2,1,0:T(8,128)(2,1)S(1)}, bf16[1,96,2304]{2,1,0:T(8,128)(2,1)S(1)}, u32[]{:S(2)}, u32[]{:S(2)}) %collective-permute-start.6) | collective-permute-done | bytes 442400 | tf_op jit(solution)/shard_map/ppermute | solution.py:25
  73.4 11.5 %attend.2 = (bf16[704,768]{1,0:T(8,128)(2,1)}, f32[704,768]{1,0:T(8,128)}) custom-call(bf16[704,768]{1,0:T(8,128)(2,1)} %add_convert_fusion.3.refs_0_, bf16[704,1536]{1,0:T(8,128)(2,1)} %copy-done.17, bf16[704,1536]{1,0:T(8,128)(2,1)} %copy-done.18, bf16[704,1536]{1,0:T(8,128)(2,1)} %copy-done.17, bf16[704,1536]{1,0:T(8,128)(2,1)} %copy-done.18), custom_call_target="tpu_custom_call" | custom-call | flops 3045064704 | bytes 4325376 | tf_op jit(solution)/shard_map/attend/pallas_call | solution.py:116
  91.4 11.1 %attend.3 = (bf16[704,768]{1,0:T(8,128)(2,1)}, f32[704,768]{1,0:T(8,128)}) custom-call(bf16[704,768]{1,0:T(8,128)(2,1)} %add_convert_fusion.3.refs_0_, bf16[704,1536]{1,0:T(8,128)(2,1)} %copy-done.17, bf16[704,1536]{1,0:T(8,128)(2,1)} %copy-done.18, bf16[704,1536]{1,0:T(8,128)(2,1)} %copy-done.17, ...), custom_call_target="tpu_custom_call", output_to_operand_aliasing={{0}: (5, {}), {1}: (6, {})} | custom-call | flops 3045064704 | bytes 4325376 | tf_op jit(solution)/shard_map/attend/pallas_call | solution.py:116
  124.7 8.8 %fusion.4 = (bf16[704,3072]{1,0:T(8,128)(2,1)}, bf16[704,3072]{1,0:T(8,128)(2,1)S(1)}) fusion(f32[3072]{0:T(1024)S(1)} %copy-done.83, bf16[768,3072]{1,0:T(8,128)(2,1)S(1)} %get-tuple-element.240, f32[704,768]{1,0:T(8,128)S(1)} %get-tuple-element.520, f32[768]{0:T(1024)S(1)} %copy-done.87, f32[768]{0:T(1024)S(1)} %copy-done.82, f32[704]{0:T(1024)S(1)} %add_rsqrt_fusion, ...), kind=kOutput, calls=%fused_computation.5 | convolution fusion | flops 3350544384 | bytes 15556096 | tf_op jit(solution)/shard_map/dot_general | solution.py:68
  135.1 4.3 convolution_convert_fusion.3
  142.2 5.1 %collective-permute-done.23.refs_5_ = bf16[2,1,384,768]{3,2,1,0:T(8,128)(2,1)S(1)} collective-permute-done((bf16[2,1,384,768]{3,2,1,0:T(8,128)(2,1)S(1)}, bf16[2,1,384,768]{3,2,1,0:T(8,128)(2,1)S(1)}, u32[]{:S(2)}, u32[]{:S(2)}) %collective-permute-start.23) | collective-permute-done | bytes 1179680 | tf_op jit(solution)/shard_map/ppermute | solution.py:25
  155.5 5.0 %convolution_convert_fusion.2 = bf16[768,3072]{1,0:T(8,128)(2,1)S(1)} fusion(bf16[704,3072]{1,0:T(8,128)(2,1)S(1)} %get-tuple-element.252, f32[704,768]{1,0:T(8,128)S(1)} %copy-done.20, f32[768]{0:T(1024)S(1)} %copy-done.87, f32[768]{0:T(1024)S(1)} %copy-done.82, f32[704]{0:T(1024)S(1)} %add_rsqrt_fusion, f32[704]{0:T(1024)S(1)} %broadcast_multiply_fusion.5), kind=kOutput, calls=%fused_computation.12 | convolution fusion | flops 3326951424 | bytes 11218432 | tf_op jit(solution)/shard_map/dot_general | solution.py:76
  161.0 4.2 fusion.12
  165.2 4.0 multiply_reduce_fusion
  175.2 14.2 %attend_back.2 = (bf16[704,768]{1,0:T(8,128)(2,1)}, bf16[2,704,768]{2,1,0:T(8,128)(2,1)}, bf16[2,704,768]{2,1,0:T(8,128)(2,1)}) custom-call(bf16[704,768]{1,0:T(8,128)(2,1)} %add_convert_fusion.3.refs_0_, bf16[704,1536]{1,0:T(8,128)(2,1)} %copy-done.17, bf16[704,1536]{1,0:T(8,128)(2,1)} %copy-done.18, bf16[704,1536]{1,0:T(8,128)(2,1)} %copy-done.17, ...), custom_call_target="tpu_custom_call" | custom-call | flops 5075107840 | bytes 4685824 | tf_op jit(solution)/shard_map/attend_back/pallas_call | solution.py:178
  189.4 4.2 collective-permute-done.24
  196.5 25.4 %attend_back.3 = (bf16[704,768]{1,0:T(8,128)(2,1)}, bf16[2,704,768]{2,1,0:T(8,128)(2,1)}, bf16[2,704,768]{2,1,0:T(8,128)(2,1)}) custom-call(bf16[704,768]{1,0:T(8,128)(2,1)} %add_convert_fusion.3.refs_0_, bf16[704,1536]{1,0:T(8,128)(2,1)} %copy-done.17, bf16[704,1536]{1,0:T(8,128)(2,1)} %copy-done.18, ...), custom_call_target="tpu_custom_call", output_to_operand_aliasing={{0}: (7, {}), {1}: (8, {}), {2}: (9, {})} | custom-call | flops 10150215680 | bytes 9371648 | tf_op jit(solution)/shard_map/attend_back/pallas_call | solution.py:178
  232.7 8.3 %multiply_convert_fusion.5 = bf16[704,768]{1,0:T(8,128)(2,1)} fusion(f32[704,768]{1,0:T(8,128)S(1)} %copy-done.20, bf16[704,3072]{1,0:T(8,128)(2,1)} %copy-done.101, bf16[3072,768]{1,0:T(8,128)(2,1)} %copy-done, f32[768]{0:T(1024)S(1)} %convert_element_type.701, f32[]{:T(128)S(6)} %convert_element_type.681), kind=kOutput, calls=%fused_computation.68 | convolution fusion | flops 3324051456 | bytes 12291076 | tf_op jit(solution)/shard_map/dot_general | solution.py:68
  245.7 4.0 convolution_convert_fusion.1
  268.1 12.0 %collective-permute-done.29 = bf16[2,2,192,768]{3,2,1,0:T(8,128)(2,1)S(1)} collective-permute-done((bf16[2,2,192,768]{3,2,1,0:T(8,128)(2,1)S(1)}, bf16[2,2,192,768]{3,2,1,0:T(8,128)(2,1)S(1)}, u32[]{:S(2)}, u32[]{:S(2)}) %collective-permute-start.29) | collective-permute-done | bytes 1179680 | tf_op jit(solution)/shard_map/ppermute | solution.py:280
  295.5 4.4 concatenate.195
  317.7 4.2 collective-permute-done.37
  342.0 4.7 %collective-permute-done.43 = bf16[192,768]{1,0:T(8,128)(2,1)S(1)} collective-permute-done((bf16[192,768]{1,0:T(8,128)(2,1)}, bf16[192,768]{1,0:T(8,128)(2,1)S(1)}, u32[]{:S(2)}, u32[]{:S(2)}) %collective-permute-start.43) | collective-permute-done | bytes 294944 | tf_op jit(solution)/shard_map/ppermute | solution.py:280
  361.5 4.0 collective-permute-done.53
  375.4 6.2 %collective-permute-done.58 = bf16[2,80,384]{2,1,0:T(8,128)(2,1)S(1)} collective-permute-done((bf16[2,80,384]{2,1,0:T(8,128)(2,1)S(1)}, bf16[2,80,384]{2,1,0:T(8,128)(2,1)S(1)}, u32[]{:S(2)}, u32[]{:S(2)}) %collective-permute-start.58) | collective-permute-done | bytes 122912 | tf_op jit(solution)/shard_map/ppermute | solution.py:392
  388.3 7.8 %collective-permute-done.68 = f32[29,768]{1,0:T(8,128)S(1)} collective-permute-done((f32[29,768]{1,0:T(8,128)S(1)}, f32[29,768]{1,0:T(8,128)S(1)}, u32[]{:S(2)}, u32[]{:S(2)}) %collective-permute-start.68) | collective-permute-done | bytes 89120 | tf_op jit(solution)/shard_map/ppermute | solution.py:280
  403.6 3.9 collective-permute-done.66
  423.1 5.4 %collective-permute-done.69 = bf16[2,320,384]{2,1,0:T(8,128)(2,1)} collective-permute-done((bf16[2,320,384]{2,1,0:T(8,128)(2,1)S(1)}, bf16[2,320,384]{2,1,0:T(8,128)(2,1)}, u32[]{:S(2)}, u32[]{:S(2)}) %collective-permute-start.69) | collective-permute-done | bytes 491552 | tf_op jit(solution)/shard_map/ppermute | solution.py:280
  434.8 4.1 collective-permute-done.71
  (554 shorter events, 261.9 us)
Async XLA Ops:
  0.7 31.4 %collective-permute-start.4 = (bf16[3,192,768]{2,1,0:T(8,128)(2,1)}, bf16[3,192,768]{2,1,0:T(8,128)(2,1)S(1)}, u32[]{:S(2)}, u32[]{:S(2)}) collective-permute-start(bf16[3,192,768]{2,1,0:T(8,128)(2,1)} %refs_1_.1), channel_id=1, source_target_pairs={{0,2},{1,3},{2,0},{3,1},{4,6},{5,7},{6,4},{7,5},{8,10},{9,11},{10,... | collective-permute-start | bytes 2654216 | tf_op jit(solution)/shard_map/ppermute | solution.py:25
  3.7 51.2 %collective-permute-start.9 = (bf16[3,192,768]{2,1,0:T(8,128)(2,1)}, bf16[3,192,768]{2,1,0:T(8,128)(2,1)}, u32[]{:S(2)}, u32[]{:S(2)}) collective-permute-start(bf16[3,192,768]{2,1,0:T(8,128)(2,1)} %refs_1_.1), channel_id=1, source_target_pairs={{0,1},{1,0},{2,3},{3,2},{4,5},{5,4},{6,7},{7,6},{8,9},{9,8},{10,11... | collective-permute-start | bytes 2654216 | tf_op jit(solution)/shard_map/ppermute | solution.py:25
  5.8 23.0 %collective-permute-start.1 = (bf16[352,160]{1,0:T(8,128)(2,1)}, bf16[352,160]{1,0:T(8,128)(2,1)}, u32[]{:S(2)}, u32[]{:S(2)}) collective-permute-start(bf16[352,160]{1,0:T(8,128)(2,1)} %get-tuple-element.503), channel_id=1, source_target_pairs={{0,0},{1,2},{2,1},{3,3},{4,4},{5,6},{6,5},{7,7},{8,8},{9,10},{10,9... | collective-permute-start | bytes 337928 | tf_op jit(solution)/shard_map/ppermute | solution.py:25
  8.8 20.1 %collective-permute-start.2 = (bf16[352,160]{1,0:T(8,128)(2,1)}, bf16[352,160]{1,0:T(8,128)(2,1)}, u32[]{:S(2)}, u32[]{:S(2)}) collective-permute-start(bf16[352,160]{1,0:T(8,128)(2,1)} %get-tuple-element.504), channel_id=1, source_target_pairs={{0,2},{1,0},{2,3},{3,1},{4,6},{5,4},{6,7},{7,5},{8,10},{9,8},{10,1... | collective-permute-start | bytes 337928 | tf_op jit(solution)/shard_map/ppermute | solution.py:25
  68.9 18.9 %collective-permute-start.13 = (bf16[5,96,768]{2,1,0:T(8,128)(2,1)}, bf16[5,96,768]{2,1,0:T(8,128)(2,1)S(1)}, u32[]{:S(2)}, u32[]{:S(2)}) collective-permute-start(bf16[5,96,768]{2,1,0:T(8,128)(2,1)} %constant_dynamic-slice_fusion.1), channel_id=1, source_target_pairs={{0,2},{1,3},{2,0},{3,1},{4,6},{5,7},{6,4},{7,5},{8,10},{9,11},{10,... | collective-permute-start | bytes 2211848 | tf_op jit(solution)/shard_map/ppermute | solution.py:25
  87.9 18.9 %collective-permute-start.14 = (bf16[5,192,768]{2,1,0:T(8,128)(2,1)S(1)}, bf16[5,192,768]{2,1,0:T(8,128)(2,1)}, u32[]{:S(2)}, u32[]{:S(2)}) collective-permute-start(bf16[5,192,768]{2,1,0:T(8,128)(2,1)S(1)} %bitcast_dynamic-update-slice_fusion.refs_1_), channel_id=1, source_target_pairs={{0,1},{1,0},{2,3},{3,2},{4,5},{5,4},{6,7},{7,6},{8,9},{9,8},{10,11... | collective-permute-start | bytes 4423688 | tf_op jit(solution)/shard_map/ppermute | solution.py:25
  87.9 18.9 %collective-permute-start.17 = (bf16[1,768,768]{2,1,0:T(8,128)(2,1)}, bf16[1,768,768]{2,1,0:T(8,128)(2,1)}, u32[]{:S(2)}, u32[]{:S(2)}) collective-permute-start(bf16[1,768,768]{2,1,0:T(8,128)(2,1)} %bitcast.21.refs_1_), channel_id=1, source_target_pairs={{0,1},{1,0},{2,3},{3,2},{4,5},{5,4},{6,7},{7,6},{8,9},{9,8},{10,11... | collective-permute-start | bytes 3538952 | tf_op jit(solution)/shard_map/ppermute | solution.py:25
  88.4 18.4 %collective-permute-start.15 = (bf16[5,96,768]{2,1,0:T(8,128)(2,1)S(1)}, bf16[5,96,768]{2,1,0:T(8,128)(2,1)S(1)}, u32[]{:S(2)}, u32[]{:S(2)}) collective-permute-start(bf16[5,96,768]{2,1,0:T(8,128)(2,1)S(1)} %collective-permute-done.13.refs_3_), channel_id=1, source_target_pairs={{0,4},{4,0},{8,12},{12,8},{16,20},{20,16},{24,28},{28,24},{1,5},{5... | collective-permute-start | bytes 2211848 | tf_op jit(solution)/shard_map/ppermute | solution.py:280
  112.3 21.2 %collective-permute-start.19 = (bf16[1,384,768]{2,1,0:T(8,128)(2,1)S(1)}, bf16[1,384,768]{2,1,0:T(8,128)(2,1)S(1)}, u32[]{:S(2)}, u32[]{:S(2)}) collective-permute-start(bf16[1,384,768]{2,1,0:T(8,128)(2,1)S(1)} %collective-permute-done.16.refs_3_), channel_id=1, source_target_pairs={{0,4},{4,0},{8,12},{12,8},{16,20},{20,16},{24,28},{28,24},{1,5},{5... | collective-permute-start | bytes 1769480 | tf_op jit(solution)/shard_map/ppermute | solution.py:280
  115.2 18.3 %collective-permute-start.20 = (bf16[352,768]{1,0:T(8,128)(2,1)S(1)}, bf16[352,768]{1,0:T(8,128)(2,1)S(1)}, u32[]{:S(2)}, u32[]{:S(2)}) collective-permute-start(bf16[352,768]{1,0:T(8,128)(2,1)S(1)} %get-tuple-element.490), channel_id=1, source_target_pairs={{0,0},{1,2},{2,1},{3,3},{4,4},{5,6},{6,5},{7,7},{8,8},{9,10},{10,9... | collective-permute-start | bytes 1622024 | tf_op jit(solution)/shard_map/ppermute | solution.py:25
  116.0 17.6 %collective-permute-start.21 = (bf16[352,768]{1,0:T(8,128)(2,1)S(1)}, bf16[352,768]{1,0:T(8,128)(2,1)S(1)}, u32[]{:S(2)}, u32[]{:S(2)}) collective-permute-start(bf16[352,768]{1,0:T(8,128)(2,1)S(1)} %get-tuple-element.489), channel_id=1, source_target_pairs={{0,2},{1,0},{2,3},{3,1},{4,6},{5,4},{6,7},{7,5},{8,10},{9,8},{10,1... | collective-permute-start | bytes 1622024 | tf_op jit(solution)/shard_map/ppermute | solution.py:25
  165.2 28.3 %collective-permute-start.24 = (bf16[768,768]{1,0:T(8,128)(2,1)}, bf16[768,768]{1,0:T(8,128)(2,1)}, u32[]{:S(2)}, u32[]{:S(2)}) collective-permute-start(bf16[768,768]{1,0:T(8,128)(2,1)} %fusion.12), channel_id=1, source_target_pairs={{0,2},{1,3},{2,0},{3,1},{4,6},{5,7},{6,4},{7,5},{8,10},{9,11},{10,... | collective-permute-start | bytes 3538952 | tf_op jit(solution)/shard_map/ppermute | solution.py:25
  196.2 27.5 %collective-permute-start.26 = (bf16[192,3072]{1,0:T(8,128)(2,1)}, bf16[192,3072]{1,0:T(8,128)(2,1)}, u32[]{:S(2)}, u32[]{:S(2)}) collective-permute-start(bf16[192,3072]{1,0:T(8,128)(2,1)} %fusion.11), channel_id=1, source_target_pairs={{0,2},{1,3},{2,0},{3,1},{4,6},{5,7},{6,4},{7,5},{8,10},{9,11},{10,... | collective-permute-start | bytes 3538952 | tf_op jit(solution)/shard_map/ppermute | solution.py:25
  223.7 17.3 %collective-permute-start.27 = (bf16[2,704,768]{2,1,0:T(8,128)(2,1)}, bf16[2,704,768]{2,1,0:T(8,128)(2,1)}, u32[]{:S(2)}, u32[]{:S(2)}) collective-permute-start(bf16[2,704,768]{2,1,0:T(8,128)(2,1)} %get-tuple-element.274), channel_id=1, source_target_pairs={{0,1},{1,0},{2,3},{3,2},{4,5},{5,4},{6,7},{7,6},{8,9},{9,8},{10,11... | collective-permute-start | bytes 6488072 | tf_op jit(solution)/shard_map/ppermute | solution.py:25
  252.2 28.0 %collective-permute-start.29 = (bf16[2,2,192,768]{3,2,1,0:T(8,128)(2,1)S(1)}, bf16[2,2,192,768]{3,2,1,0:T(8,128)(2,1)S(1)}, u32[]{:S(2)}, u32[]{:S(2)}) collective-permute-start(bf16[2,2,192,768]{3,2,1,0:T(8,128)(2,1)S(1)} %dynamic-slice_bitcast_fusion.4), channel_id=1, source_target_pairs={{0,4},{4,0},{8,12},{12,8},{16,20},{20,16},{24,28},{28,24},{1,5},{5... | collective-permute-start | bytes 3538952 | tf_op jit(solution)/shard_map/ppermute | solution.py:280
  254.0 26.1 %collective-permute-start.30 = (bf16[352,768]{1,0:T(8,128)(2,1)S(1)}, bf16[352,768]{1,0:T(8,128)(2,1)S(1)}, u32[]{:S(2)}, u32[]{:S(2)}) collective-permute-start(bf16[352,768]{1,0:T(8,128)(2,1)S(1)} %get-tuple-element.488), channel_id=1, source_target_pairs={{0,0},{2,1},{1,2},{3,3},{4,4},{6,5},{5,6},{7,7},{8,8},{10,9},{9,10... | collective-permute-start | bytes 1622024 | tf_op jit(solution)/shard_map/ppermute | solution.py:25
  254.8 25.3 %collective-permute-start.31 = (bf16[352,768]{1,0:T(8,128)(2,1)S(1)}, bf16[352,768]{1,0:T(8,128)(2,1)S(1)}, u32[]{:S(2)}, u32[]{:S(2)}) collective-permute-start(bf16[352,768]{1,0:T(8,128)(2,1)S(1)} %get-tuple-element.487), channel_id=1, source_target_pairs={{2,0},{0,1},{3,2},{1,3},{6,4},{4,5},{7,6},{5,7},{10,8},{8,9},{11,1... | collective-permute-start | bytes 1622024 | tf_op jit(solution)/shard_map/ppermute | solution.py:25
  281.3 18.6 %collective-permute-start.33 = (bf16[2,192,768]{2,1,0:T(8,128)(2,1)}, bf16[2,192,768]{2,1,0:T(8,128)(2,1)}, u32[]{:S(2)}, u32[]{:S(2)}) collective-permute-start(bf16[2,192,768]{2,1,0:T(8,128)(2,1)} %fusion.35), channel_id=1, source_target_pairs={{0,8},{4,12},{8,0},{12,4},{16,24},{20,28},{24,16},{28,20},{1,9},{5... | collective-permute-start | bytes 1769480 | tf_op jit(solution)/shard_map/ppermute | solution.py:280
  288.4 29.3 %collective-permute-start.36 = (bf16[2,2,2,24,1536]{4,3,2,1,0:T(8,128)(2,1)}, bf16[2,2,2,24,1536]{4,3,2,1,0:T(8,128)(2,1)}, u32[]{:S(2)}, u32[]{:S(2)}) collective-permute-start(bf16[2,2,2,24,1536]{4,3,2,1,0:T(8,128)(2,1)} %fusion.33), channel_id=1, source_target_pairs={{0,4},{4,0},{8,12},{12,8},{16,20},{20,16},{24,28},{28,24},{1,5},{5... | collective-permute-start | bytes 1769480 | tf_op jit(solution)/shard_map/ppermute | solution.py:280
  289.9 27.8 %collective-permute-start.35 = (bf16[2,2,2,24,1536]{4,3,2,1,0:T(8,128)(2,1)}, bf16[2,2,2,24,1536]{4,3,2,1,0:T(8,128)(2,1)}, u32[]{:S(2)}, u32[]{:S(2)}) collective-permute-start(bf16[2,2,2,24,1536]{4,3,2,1,0:T(8,128)(2,1)} %fusion.34), channel_id=1, source_target_pairs={{0,2},{1,3},{2,0},{3,1},{4,6},{5,7},{6,4},{7,5},{8,10},{9,11},{10,... | collective-permute-start | bytes 1769480 | tf_op jit(solution)/shard_map/ppermute | solution.py:25
  312.6 20.4 %collective-permute-start.40 = (bf16[2,2,2,72,384]{4,3,2,1,0:T(8,128)(2,1)}, bf16[2,2,2,72,384]{4,3,2,1,0:T(8,128)(2,1)}, u32[]{:S(2)}, u32[]{:S(2)}) collective-permute-start(bf16[2,2,2,72,384]{4,3,2,1,0:T(8,128)(2,1)} %fusion.40), channel_id=1, source_target_pairs={{0,4},{4,0},{8,12},{12,8},{16,20},{20,16},{24,28},{28,24},{1,5},{5... | collective-permute-start | bytes 1327112 | tf_op jit(solution)/shard_map/ppermute | solution.py:280
  346.9 18.6 %collective-permute-start.53 = (bf16[384,768]{1,0:T(8,128)(2,1)S(1)}, bf16[384,768]{1,0:T(8,128)(2,1)S(1)}, u32[]{:S(2)}, u32[]{:S(2)}) collective-permute-start(bf16[384,768]{1,0:T(8,128)(2,1)S(1)} %maximum_select_fusion.6), channel_id=1, source_target_pairs={{0,8},{4,12},{8,0},{12,4},{16,24},{20,28},{24,16},{28,20},{1,9},{5... | collective-permute-start | bytes 1769480 | tf_op jit(solution)/shard_map/ppermute | solution.py:280
  373.0 34.5 %collective-permute-start.67 = (bf16[768,768]{1,0:T(8,128)(2,1)S(1)}, bf16[768,768]{1,0:T(8,128)(2,1)S(1)}, u32[]{:S(2)}, u32[]{:S(2)}) collective-permute-start(bf16[768,768]{1,0:T(8,128)(2,1)S(1)} %maximum_select_fusion.1), channel_id=1, source_target_pairs={{0,4},{4,0},{8,12},{12,8},{16,20},{20,16},{24,28},{28,24},{1,5},{5... | collective-permute-start | bytes 3538952 | tf_op jit(solution)/shard_map/ppermute | solution.py:280
  387.7 19.8 %collective-permute-start.61 = (bf16[2,24,1536]{2,1,0:T(8,128)(2,1)}, bf16[2,24,1536]{2,1,0:T(8,128)(2,1)}, u32[]{:S(2)}, u32[]{:S(2)}) collective-permute-start(bf16[2,24,1536]{2,1,0:T(8,128)(2,1)} %fusion.66), channel_id=1, source_target_pairs={{0,16},{4,20},{8,24},{12,28},{16,0},{20,4},{24,8},{28,12},{1,17},{... | collective-permute-start | bytes 442376 | tf_op jit(solution)/shard_map/ppermute | solution.py:392
  (152 other events, 1231.5 us)
